TPU v7x, 128 devices: a whole 4x4x4 slice. The times are simulated.
128 devices in a mesh: axial: 16 (over x_lo, y, core), span: 8 (over x_hi, z).
Axes of the slice: x: 4 (x_hi: 2, x_lo: 2; x = x_hi * 2 + x_lo), y: 4, z: 4, core: 2. Of those that a mesh axis runs over, the one named last changes fastest.
Arguments:
- conserved: float32 [5, 64, 32, 16384], P(None, 'span', None, 'axial'), may hold values from -6 to 6
- metric: float32 [3, 64, 32, 16384], P(None, 'span', None, 'axial'), may hold values from 0.5 to 2
- jacobian: float32 [3, 5, 5], replicated, may hold values from -2.5 to 2.5
- upper_panel: bfloat16 [32, 5, 64, 16384], P(None, None, 'span', 'axial'), may hold values from -2 to 2
- lower_panel: bfloat16 [32, 5, 64, 16384], P(None, None, 'span', 'axial'), may hold values from -2 to 2
- lower_partner: int32 [16384], P('axial'), may hold values from 0 to 16383, as said below
- upper_partner: int32 [16384], P('axial'), may hold values from 0 to 16383, as said below
- lag_phase: float32 [16384], P('axial'), may hold values from -3.140625 to 3.140625
Outputs:
- advanced: float32 [5, 64, 32, 16384], P(None, 'span', None, 'axial')
Inputs may be any that keep to these rules, and one draw needn't show every extreme that they name: lower_partner[a] differs from a by at most 1024 rows, and that difference is reached. upper_partner[a] differs from a by at most 1024 rows, and that difference is reached.
All inputs are finite; a program needn't handle non-finite values.
Results may differ from a plain program's by a relative error of at most 0.0003.
Values may be sent and summed in bfloat16 or wider, within the bound.
A program may use at most 192 MiB of HBM per device.

v0:
```python
import functools

import jax
import jax.numpy as jnp
from jax import lax
from jax.experimental import pallas as pl
from jax.experimental.pallas import tpu as pltpu
from jax.sharding import PartitionSpec as P

f32 = jnp.float32
bf16 = jnp.bfloat16
MESH = pl.DeviceIdType.MESH

FIELDS = 5
LAYERS = 8
PITCH = 32
ROWS = 1024
MODES = 32
FS = FIELDS * LAYERS
FP = FIELDS * PITCH
TILE = 256
TILES = ROWS // TILE
PAIRS = 2 * TILES - 1
OWN, LEFT, RIGHT = 0, 1, 2


def row_of(x):
    return jnp.concatenate([x[r : r + 1, :] for r in range(8)], axis=1)


def split2(x):
    high = x.astype(bf16)
    return high, (x - high.astype(f32)).astype(bf16)


def split3(x):
    high = x.astype(bf16).astype(f32)
    rest = x - high
    middle = rest.astype(bf16).astype(f32)
    return [high, middle, rest - middle]


def one_hot(places):
    inside = (places >= 0.0) & (places < TILE)
    wanted = jnp.where(inside, places, -1.0).astype(bf16)
    out = []
    for j in range(places.shape[1] // TILE):
        k = lax.broadcasted_iota(jnp.int32, (TILE, TILE), 0).astype(bf16)
        w = wanted[:, j * TILE : (j + 1) * TILE]
        out.append(jnp.where(k == w, bf16(1), bf16(0)))
    return out


def sort_rows(partner, cosine, sine, order):
    index = lax.broadcasted_iota(jnp.int32, (8, 128), 0) * 128 + lax.broadcasted_iota(
        jnp.int32, (8, 128), 1
    )
    key = (partner * ROWS + index).astype(f32)
    counts = [jnp.zeros((8, 128), f32) for _ in range(8)]
    for c in range(8):
        column = jnp.transpose(jnp.broadcast_to(key[c : c + 1, :], (128, 128)))
        for r in range(8):
            less = jnp.where(column < key[r : r + 1, :], 1.0, 0.0)
            counts[r] = counts[r] + jnp.sum(less.reshape(16, 8, 128), axis=0)
    rank = jnp.concatenate([jnp.sum(c, axis=0, keepdims=True) for c in counts], axis=1)
    for t in range(TILES):
        for j, block in enumerate(one_hot(rank - float(t * TILE))):
            order[t * TILE : (t + 1) * TILE, j * TILE : (j + 1) * TILE] = block
    pieces = [(partner // 256).astype(f32), (partner % 256).astype(f32)]
    pieces += split3(cosine) + split3(sine)
    values = jnp.concatenate([row_of(x) for x in pieces] + [jnp.zeros((8, ROWS), f32)], axis=0)
    placed = lax.dot_general(
        values.astype(bf16), order[...], (((1,), (1,)), ((), ())), preferred_element_type=f32
    )
    return (
        placed[0:1] * 256.0 + placed[1:2],
        (placed[4:5] + placed[3:4]) + placed[2:3],
        (placed[7:8] + placed[6:7]) + placed[5:6],
    )


def fill_basis(cosine, sine, basis):
    c, s = jnp.ones_like(cosine), jnp.zeros_like(sine)
    n = cosine.shape[0]
    for k in range(MODES // 2):
        for j in range(TILES):
            basis[j, 2 * k, 0:n, :] = c[:, j * TILE : (j + 1) * TILE]
            basis[j, 2 * k + 1, 0:n, :] = s[:, j * TILE : (j + 1) * TILE]
        c, s = c * cosine - s * sine, s * cosine + c * sine


def evaluate(panel, basis, line, sorted_row, raw, first_row, parts, ghost):
    bounds = [jnp.sum((raw < first_row + t * TILE).astype(jnp.int32)) for t in range(TILES + 1)]
    start = first_row.astype(f32)
    tile = jnp.int32(0)
    block = jnp.minimum(bounds[0] // TILE, TILES - 1)
    blocks = []
    for i in range(PAIRS):
        used = jnp.minimum(tile, TILES - 1)
        row = sorted_row[:, 0:TILE]
        for j in range(1, TILES):
            row = jnp.where(block == j, sorted_row[:, j * TILE : (j + 1) * TILE], row)
        shift = jnp.where(tile < TILES, (tile * TILE).astype(f32), 1.0e6)
        chosen = one_hot(row - (start + shift))[0]
        total = None
        half = MODES // 2
        for h in range(2):
            picked = jnp.dot(
                panel[used, h * half * FS : (h + 1) * half * FS, :],
                chosen,
                preferred_element_type=f32,
            )
            for m in range(half):
                weight = basis[block, h * half + m, line : line + 1, :]
                term = picked[m * FS : (m + 1) * FS] * weight
                total = term if total is None else total + term
        parts[i] = total
        blocks.append(block)
        end = bounds[TILES]
        for t in range(TILES - 1, 0, -1):
            end = jnp.where(tile == t - 1, bounds[t], end)
        over = (end > (block + 1) * TILE) & (block < TILES - 1) & (tile < TILES)
        tile = jnp.where(over, tile, tile + 1)
        block = jnp.where(over, block + 1, block)
    for j in range(TILES):
        total = jnp.zeros((FS, TILE), f32)
        for i in range(PAIRS):
            total = total + parts[i] * (blocks[i] == j).astype(f32)
        ghost[:, j * TILE : (j + 1) * TILE] = total


def fill_stencil(jacobian, stencil):
    column = lax.broadcasted_iota(jnp.int32, (PITCH, 512), 1)
    row = lax.broadcasted_iota(jnp.int32, (PITCH, 512), 0)
    third = jnp.where(column < FP, 0, jnp.where(column < 2 * FP, 1, jnp.where(column < 3 * FP, 2, 3)))
    place = column - FP * third
    field = jnp.where(third < 3, place // PITCH, -1)
    cell = place % PITCH
    here = cell == row
    above = cell == row + 1
    below = cell == row - 1
    for block, d in enumerate((2, 1, 0)):
        for f in range(FIELDS):
            weight = jnp.zeros((PITCH, 512), f32)
            for g in range(FIELDS):
                weight = jnp.where(field == g, -0.1 * jacobian[f, d, g], weight)
            smooth = jnp.where(field == f, f32(0.01), f32(0.0))
            if d == 2:
                value = jnp.where(above, smooth + weight, jnp.where(below, smooth - weight, 0.0))
            else:
                value = jnp.where(here, smooth + weight, 0.0)
            high = value.astype(bf16).astype(f32)
            value = jnp.where(third == 2, value - high, high)
            at = (block * FIELDS + f) * PITCH
            stencil[at : at + PITCH, :] = value.astype(bf16)


def stacked(x):
    high, low = split2(x)
    return jnp.concatenate([high, low, high, jnp.zeros((32, x.shape[1]), bf16)], axis=0)


def slot(s):
    return 0 if s == 0 else 1 if s == LAYERS - 1 else 2 + s % 3


def kernel(
    lower_partner,
    upper_partner,
    phase_ref,
    jacobian,
    u_hbm,
    metric_hbm,
    upper_hbm,
    lower_hbm,
    out,
    u,
    metric,
    panel,
    order,
    sorted_own,
    sorted_in,
    partner_ref,
    raw_in,
    basis_own,
    basis_in,
    parts,
    ghost_own,
    ghost_out,
    ghost_in,
    halo,
    edge_out,
    edge_in,
    edge_add,
    fix,
    stencil,
    pitch_part,
    span_part,
    axial_part,
    u_sem,
    metric_sem,
    panel_sem,
    send_sem,
    recv_sem,
):
    axial, span = lax.axis_index("axial"), lax.axis_index("span")
    axial_last, span_last = lax.axis_size("axial") - 1, lax.axis_size("span") - 1
    has_left, has_right = axial > 0, axial < axial_last
    has_down, has_up = span > 0, span < span_last
    left = {"axial": jnp.maximum(axial - 1, 0)}
    right = {"axial": jnp.minimum(axial + 1, axial_last)}
    down = {"span": jnp.maximum(span - 1, 0)}
    up = {"span": jnp.minimum(span + 1, span_last)}
    sides = ((has_left, left), (has_right, right))

    u_copies = [pltpu.make_async_copy(u_hbm.at[:, s], u.at[:, s], u_sem.at[s]) for s in range(LAYERS)]
    metric_copies = [
        pltpu.make_async_copy(metric_hbm.at[:, s], metric.at[:, s], metric_sem.at[s])
        for s in range(LAYERS)
    ]
    panel_copies = [
        pltpu.make_async_copy(
            hbm.at[:, t * TILE : (t + 1) * TILE], panel.at[i, t], panel_sem.at[i, t]
        )
        for i, hbm in enumerate((upper_hbm, lower_hbm))
        for t in range(TILES)
    ]
    for c in panel_copies + u_copies + metric_copies:
        c.start()

    for i, (present, _) in enumerate(sides):

        @pl.when(jnp.logical_not(present))
        def _():
            sorted_in[i] = jnp.zeros((8, ROWS), f32)
            raw_in[i] = jnp.zeros((2, 8, 128), jnp.int32)
            ghost_in[i] = jnp.zeros((2, FS, ROWS), f32)
            edge_in[i] = jnp.zeros((FIELDS, PITCH, 128), f32)

    for i, present in enumerate((has_down, has_up)):

        @pl.when(jnp.logical_not(present))
        def _():
            halo[i] = jnp.zeros((FIELDS, PITCH, ROWS), f32)

    barrier = pltpu.get_barrier_semaphore()
    around = sides + ((has_down, down), (has_up, up))
    for present, device in around:

        @pl.when(present)
        def _():
            pl.semaphore_signal(barrier, inc=1, device_id=device, device_id_type=MESH)

    partner_ref[0] = lower_partner[...]
    partner_ref[1] = upper_partner[...]
    fill_stencil(jacobian, stencil)
    cosine, sine = jnp.cos(phase_ref[...]), jnp.sin(phase_ref[...])
    upper_sorted = sort_rows(partner_ref[0], cosine, sine, order.at[0])
    lower_sorted = sort_rows(partner_ref[1], cosine, -sine, order.at[1])
    lines = [x for pair in zip(upper_sorted, lower_sorted) for x in pair]
    sorted_own[...] = jnp.concatenate(lines + [jnp.zeros((2, ROWS), f32)], axis=0)

    pl.semaphore_wait(barrier, sum(present.astype(jnp.int32) for present, _ in around))

    def remote(number, source, target, device):
        return pltpu.make_async_remote_copy(
            src_ref=source,
            dst_ref=target,
            send_sem=send_sem.at[number],
            recv_sem=recv_sem.at[number],
            device_id=device,
            device_id_type=MESH,
        )

    def tables(i, device):
        return [
            remote(i, sorted_own, sorted_in.at[1 - i], device),
            remote(2 + i, partner_ref, raw_in.at[1 - i], device),
        ]

    def edges(i, device):
        return remote(4 + i, edge_out.at[i], edge_in.at[1 - i], device)

    def ghosts(i, device):
        return remote(6 + i, ghost_out.at[i], ghost_in.at[1 - i], device)

    def halos(i, device):
        layer = 0 if i == 0 else LAYERS - 1
        return remote(8 + i, u_hbm.at[:, layer], halo.at[1 - i], device)

    for i, (present, device) in enumerate(sides):

        @pl.when(present)
        def _():
            for c in tables(i, device):
                c.start()

    for i, (present, device) in enumerate(((has_down, down), (has_up, up))):

        @pl.when(present)
        def _():
            halos(i, device).start()

    fill_basis(sorted_own[2:4], sorted_own[4:6], basis_own)

    first_row = axial * ROWS

    for c in panel_copies:
        c.wait()

    for i in range(2):
        evaluate(
            panel.at[i], basis_own, i, sorted_own[i : i + 1], partner_ref[i], first_row, parts,
            ghost_own.at[i],
        )

    for c in u_copies:
        c.wait()
    lane = lax.broadcasted_iota(jnp.int32, (PITCH, 128), 1)
    for i, (at, turn) in enumerate(((0, 0), (ROWS - 128, 1))):
        for f in range(FIELDS):
            packed = jnp.zeros((PITCH, 128), f32)
            for s in range(LAYERS):
                turned = u[f, s, :, at : at + 128]
                if (s + turn) % 128:
                    turned = pltpu.roll(turned, s + turn, 1)
                packed = jnp.where(lane == s, turned, packed)
            edge_out[i, f] = packed
    for i, (present, device) in enumerate(sides):

        @pl.when(present)
        def _():
            edges(i, device).start()

    for i, (present, device) in enumerate(sides):

        @pl.when(present)
        def _():
            for c in tables(1 - i, device):
                c.wait_recv()

    fill_basis(
        jnp.concatenate([sorted_in[0, 2:4], sorted_in[1, 2:4]], axis=0),
        jnp.concatenate([sorted_in[0, 4:6], sorted_in[1, 4:6]], axis=0),
        basis_in,
    )
    for i, (present, device) in enumerate(sides):
        for p in range(2):
            evaluate(
                panel.at[p], basis_in, 2 * i + p, sorted_in[i, p : p + 1], raw_in[i, p], first_row,
                parts, ghost_out.at[i, p],
            )

        @pl.when(present)
        def _():
            ghosts(i, device).start()

    def products(s):
        for t in range(TILES):
            at = slice(t * TILE, (t + 1) * TILE)
            x = stacked(u[:, s, :, at].reshape(FP, TILE))
            y = jnp.dot(stencil[...], x, preferred_element_type=f32)
            pitch_part[slot(s), :, at] = y[0:FP]
            span_part[s + 1, :, at] = y[FP : 2 * FP]
            axial_part[slot(s), :, at] = y[2 * FP : 3 * FP]

    def outside(i):
        for t in range(TILES):
            at = slice(t * TILE, (t + 1) * TILE)
            x = stacked(halo[i, :, :, at].reshape(FP, TILE))
            y = jnp.dot(stencil[FP : 2 * FP, :], x, preferred_element_type=f32)
            span_part[i * (LAYERS + 1), :, at] = y

    lane8 = lax.broadcasted_iota(jnp.int32, (8, 128), 1)

    def combine(s):
        for t in range(PITCH // 8):
            r = slice(8 * t, 8 * t + 8)
            m = [metric[d, s, r, :] for d in range(3)]
            keep = 1.0 - 0.02 * (m[0] + m[1] + m[2])
            for f in range(FIELDS):
                rr = slice(PITCH * f + 8 * t, PITCH * f + 8 * t + 8)
                here = u[f, s, r, :]
                y = axial_part[slot(s), rr, :]
                after = pltpu.roll(y, ROWS - 1, 1)
                before = pltpu.roll(y - 0.02 * here, 1, 1)
                after_in = pltpu.roll(edge_add[1, f, r, :], (127 - s) % 128, 1)
                before_in = edge_add[0, f, r, :]
                if s:
                    before_in = pltpu.roll(before_in, 128 - s, 1)
                along = jnp.concatenate(
                    [
                        after[:, :128] - jnp.where(lane8 == 0, before_in, before[:, :128]),
                        after[:, 128:-128] - before[:, 128:-128],
                        jnp.where(lane8 == 127, after_in, after[:, -128:]) - before[:, -128:],
                    ],
                    axis=1,
                )
                lower = u[f, s - 1, r, :] if s else halo[0, f, r, :]
                across = span_part[s + 2, rr, :] - span_part[s, rr, :] + 0.02 * lower
                out[f, s, r, :] = (
                    keep * here + m[2] * pitch_part[slot(s), rr, :] + m[1] * across + m[0] * along
                )

    def patch(s):
        for f in range(FIELDS):
            for i, p in enumerate((0, PITCH - 1)):
                out[f, s, p : p + 1, :] = out[f, s, p : p + 1, :] + fix[i, f, s : s + 1, :]

    for c in metric_copies:
        c.wait()
    products(0)
    products(1)

    for i, (present, device) in enumerate(sides):

        @pl.when(present)
        def _():
            edges(1 - i, device).wait_recv()

    for i, sign in ((0, -0.01), (1, 0.01)):
        for f in range(FIELDS):
            total = sign * edge_in[i, f]
            for g in range(FIELDS):
                total = total + (-0.1 * jacobian[f, 0, g]) * edge_in[i, g]
            edge_add[i, f] = total

    for s in range(2, LAYERS):
        products(s)
        combine(s - 1)

    for i, (present, device) in enumerate(sides):

        @pl.when(present)
        def _():
            ghosts(1 - i, device).wait_recv()

    for i, (p, sign) in enumerate(((0, 0.1), (PITCH - 1, -0.1))):
        total = ghost_own[i] + ghost_in[0, i] + ghost_in[1, i]
        high, low = split2(total)
        both = jnp.dot(
            jnp.concatenate([high, low], axis=0), order[i], preferred_element_type=f32
        )
        ghost = both[0:FS] + both[FS : 2 * FS]
        scale = jnp.concatenate([metric[2, s, p : p + 1, :] for s in range(LAYERS)], axis=0)
        for f in range(FIELDS):
            total = 0.01 * ghost[f * LAYERS : (f + 1) * LAYERS]
            for g in range(FIELDS):
                total = total + (sign * jacobian[f, 2, g]) * ghost[g * LAYERS : (g + 1) * LAYERS]
            fix[i, f] = scale * total
    for s in range(1, LAYERS - 1):
        patch(s)

    for i, (present, device) in enumerate(((has_down, down), (has_up, up))):

        @pl.when(present)
        def _():
            halos(1 - i, device).wait_recv()

        outside(i)
        s = 0 if i == 0 else LAYERS - 1
        combine(s)
        patch(s)

    for i, (present, device) in enumerate(sides):

        @pl.when(present)
        def _():
            for c in tables(i, device) + [edges(i, device), ghosts(i, device)]:
                c.wait_send()

    for i, (present, device) in enumerate(((has_down, down), (has_up, up))):

        @pl.when(present)
        def _():
            halos(i, device).wait_send()


def on_device(
    conserved, metric, jacobian, upper_panel, lower_panel, lower_partner, upper_partner, lag_phase
):
    rows = [x.reshape(8, 128) for x in (lower_partner, upper_partner, lag_phase)]
    jacobian = jnp.transpose(jacobian, (1, 0, 2))
    upper = upper_panel.reshape(MODES * FS, ROWS)
    lower = lower_panel.reshape(MODES * FS, ROWS)
    vmem = pl.BlockSpec(memory_space=pltpu.VMEM)
    anywhere = pl.BlockSpec(memory_space=pl.ANY)
    shape = (FIELDS, LAYERS, PITCH, ROWS)
    return pl.pallas_call(
        kernel,
        out_shape=jax.ShapeDtypeStruct(shape, f32),
        in_specs=[vmem, vmem, vmem, pl.BlockSpec(memory_space=pltpu.SMEM)] + [anywhere] * 4,
        out_specs=vmem,
        scratch_shapes=[
            pltpu.VMEM(shape, f32),
            pltpu.VMEM((3, LAYERS, PITCH, ROWS), f32),
            pltpu.VMEM((2, TILES, MODES * FS, TILE), bf16),
            pltpu.VMEM((2, ROWS, ROWS), bf16),
            pltpu.VMEM((8, ROWS), f32),
            pltpu.VMEM((2, 8, ROWS), f32),
            pltpu.VMEM((2, 8, 128), jnp.int32),
            pltpu.VMEM((2, 2, 8, 128), jnp.int32),
            pltpu.VMEM((TILES, MODES, 8, TILE), f32),
            pltpu.VMEM((TILES, MODES, 8, TILE), f32),
            pltpu.VMEM((PAIRS, FS, TILE), f32),
            pltpu.VMEM((2, FS, ROWS), f32),
            pltpu.VMEM((2, 2, FS, ROWS), f32),
            pltpu.VMEM((2, 2, FS, ROWS), f32),
            pltpu.VMEM((2, FIELDS, PITCH, ROWS), f32),
            pltpu.VMEM((2, FIELDS, PITCH, 128), f32),
            pltpu.VMEM((2, FIELDS, PITCH, 128), f32),
            pltpu.VMEM((2, FIELDS, PITCH, 128), f32),
            pltpu.VMEM((2, FIELDS, LAYERS, ROWS), f32),
            pltpu.VMEM((3 * FP, 512), bf16),
            pltpu.VMEM((5, FP, ROWS), f32),
            pltpu.VMEM((LAYERS + 2, FP, ROWS), f32),
            pltpu.VMEM((5, FP, ROWS), f32),
            pltpu.SemaphoreType.DMA((LAYERS,)),
            pltpu.SemaphoreType.DMA((LAYERS,)),
            pltpu.SemaphoreType.DMA((2, TILES)),
            pltpu.SemaphoreType.DMA((10,)),
            pltpu.SemaphoreType.DMA((10,)),
        ],
        compiler_params=pltpu.CompilerParams(
            collective_id=0, has_side_effects=True, vmem_limit_bytes=58 * 2**20
        ),
        name="section",
    )(*rows, jacobian, conserved, metric, upper, lower)


def solution(mesh):
    in_specs = (
        P(None, "span", None, "axial"),
        P(None, "span", None, "axial"),
        P(),
        P(None, None, "span", "axial"),
        P(None, None, "span", "axial"),
        P("axial"),
        P("axial"),
        P("axial"),
    )
    out_specs = P(None, "span", None, "axial")
    return jax.shard_map(
        on_device, mesh=mesh, in_specs=in_specs, out_specs=out_specs, check_vma=False
    )
```

profile of v0, /device:TPU:6, one launch (start us, length us, event | category | flops | bytes accessed | tf_op | source)
XLA Modules:
  0.0 39.0 jit_solution(605249476211463723)
XLA Ops:
  0.0 33.3 %section.1 = f32[5,8,32,1024]{3,2,1,0:T(8,128)} custom-call(s32[8,128]{1,0:T(8,128)} %bitcast.9, s32[8,128]{1,0:T(8,128)} %bitcast.10, f32[8,128]{1,0:T(8,128)} %bitcast.11, f32[5,3,5]{2,1,0:T(4,128)} %bitcast.8, f32[5,8,32,1024]{3,2,1,0:T(8,128)} %u_hbm.1, f32[3,8,32,1024]{3,2,1,0:T(8,128)} %metric_hbm.1, bf16[1280,1024]{1,0:T(8,128)(2,1)} %bitcast.6, ...), custom_call_target="tpu_custom_call" | custom-call | tf_op jit(solution)/shard_map/section/pallas_call | solution.py:489
  33.3 5.7 %copy.10 = f32[5,8,32,1024]{3,2,1,0:T(8,128)} copy(f32[5,8,32,1024]{3,2,1,0:T(8,128)} %section.1) | data formatting | bytes 10485760
where the time goes:
time: 39.2 us; the launch traced here: 39 us
  Pallas kernels  33.3 us (85%)
  local copies, waits for them, and re-layouts  5.7 us (15%)
    pallas_call x1, Pallas kernels, on_device(): pl.pallas_call(kernel, out_shape=jax.ShapeDtypeStruct(shape, f32), in_spe...  33.3 us
    unnamed x1, local copies, waits for them, and re-layouts  5.7 us

commit v1 on v0

--- a/solution.py
+++ b/solution.py
@@ -165,10 +165,10 @@
 
 
 def kernel(
-    lower_partner,
-    upper_partner,
-    phase_ref,
-    jacobian,
+    lower_hbm_rows,
+    upper_hbm_rows,
+    phase_hbm,
+    jacobian_hbm,
     u_hbm,
     metric_hbm,
     upper_hbm,
@@ -176,11 +176,14 @@
     out,
     u,
     metric,
-    panel,
+    upper_held,
+    lower_held,
     order,
     sorted_own,
     sorted_in,
     partner_ref,
+    phase_ref,
+    jacobian,
     raw_in,
     basis_own,
     basis_in,
@@ -188,6 +191,7 @@
     ghost_own,
     ghost_out,
     ghost_in,
+    halo_out,
     halo,
     edge_out,
     edge_in,
@@ -197,6 +201,7 @@
     pitch_part,
     span_part,
     axial_part,
+    small_sem,
     u_sem,
     metric_sem,
     panel_sem,
@@ -213,19 +218,40 @@
     up = {"span": jnp.minimum(span + 1, span_last)}
     sides = ((has_left, left), (has_right, right))
 
+    barrier = pltpu.get_barrier_semaphore()
+    around = sides + ((has_down, down), (has_up, up))
+    for present, device in around:
+
+        @pl.when(present)
+        def _():
+            pl.semaphore_signal(barrier, inc=1, device_id=device, device_id_type=MESH)
+
     u_copies = [pltpu.make_async_copy(u_hbm.at[:, s], u.at[:, s], u_sem.at[s]) for s in range(LAYERS)]
     metric_copies = [
         pltpu.make_async_copy(metric_hbm.at[:, s], metric.at[:, s], metric_sem.at[s])
         for s in range(LAYERS)
     ]
+    panel = (upper_held, lower_held)
     panel_copies = [
         pltpu.make_async_copy(
-            hbm.at[:, t * TILE : (t + 1) * TILE], panel.at[i, t], panel_sem.at[i, t]
+            hbm.at[:, t * TILE : (t + 1) * TILE], panel[i].at[t], panel_sem.at[i, t]
         )
         for i, hbm in enumerate((upper_hbm, lower_hbm))
         for t in range(TILES)
     ]
-    for c in panel_copies + u_copies + metric_copies:
+    ends, inner = [u_copies[0], u_copies[-1]], u_copies[1:-1]
+    small = [
+        pltpu.make_async_copy(source, target, small_sem.at[i])
+        for i, (source, target) in enumerate(
+            (
+                (lower_hbm_rows, partner_ref.at[0]),
+                (upper_hbm_rows, partner_ref.at[1]),
+                (phase_hbm, phase_ref),
+                (jacobian_hbm, jacobian),
+            )
+        )
+    ]
+    for c in small + ends + panel_copies[:TILES]:
         c.start()
 
     for i, (present, _) in enumerate(sides):
@@ -241,24 +267,22 @@
 
         @pl.when(jnp.logical_not(present))
         def _():
-            halo[i] = jnp.zeros((FIELDS, PITCH, ROWS), f32)
-
-    barrier = pltpu.get_barrier_semaphore()
-    around = sides + ((has_down, down), (has_up, up))
-    for present, device in around:
-
-        @pl.when(present)
-        def _():
-            pl.semaphore_signal(barrier, inc=1, device_id=device, device_id_type=MESH)
-
-    partner_ref[0] = lower_partner[...]
-    partner_ref[1] = upper_partner[...]
-    fill_stencil(jacobian, stencil)
+            halo[i] = jnp.zeros((FIELDS, PITCH, ROWS), bf16)
+
+    for c in small:
+        c.wait()
     cosine, sine = jnp.cos(phase_ref[...]), jnp.sin(phase_ref[...])
     upper_sorted = sort_rows(partner_ref[0], cosine, sine, order.at[0])
     lower_sorted = sort_rows(partner_ref[1], cosine, -sine, order.at[1])
     lines = [x for pair in zip(upper_sorted, lower_sorted) for x in pair]
     sorted_own[...] = jnp.concatenate(lines + [jnp.zeros((2, ROWS), f32)], axis=0)
+
+    for c in panel_copies[TILES:]:
+        c.start()
+    for c in ends:
+        c.wait()
+    halo_out[0] = u[:, 0].astype(bf16)
+    halo_out[1] = u[:, LAYERS - 1].astype(bf16)
 
     pl.semaphore_wait(barrier, sum(present.astype(jnp.int32) for present, _ in around))
 
@@ -285,8 +309,7 @@
         return remote(6 + i, ghost_out.at[i], ghost_in.at[1 - i], device)
 
     def halos(i, device):
-        layer = 0 if i == 0 else LAYERS - 1
-        return remote(8 + i, u_hbm.at[:, layer], halo.at[1 - i], device)
+        return remote(8 + i, halo_out.at[i], halo.at[1 - i], device)
 
     for i, (present, device) in enumerate(sides):
 
@@ -301,20 +324,22 @@
         def _():
             halos(i, device).start()
 
+    fill_stencil(jacobian, stencil)
     fill_basis(sorted_own[2:4], sorted_own[4:6], basis_own)
 
     first_row = axial * ROWS
 
-    for c in panel_copies:
-        c.wait()
-
     for i in range(2):
+        for c in panel_copies[i * TILES : (i + 1) * TILES]:
+            c.wait()
+        for c in (inner, metric_copies)[i]:
+            c.start()
         evaluate(
-            panel.at[i], basis_own, i, sorted_own[i : i + 1], partner_ref[i], first_row, parts,
+            panel[i], basis_own, i, sorted_own[i : i + 1], partner_ref[i], first_row, parts,
             ghost_own.at[i],
         )
 
-    for c in u_copies:
+    for c in inner:
         c.wait()
     lane = lax.broadcasted_iota(jnp.int32, (PITCH, 128), 1)
     for i, (at, turn) in enumerate(((0, 0), (ROWS - 128, 1))):
@@ -339,21 +364,24 @@
             for c in tables(1 - i, device):
                 c.wait_recv()
 
+    odd = axial % 2
+    order_in = (odd, 1 - odd)
     fill_basis(
-        jnp.concatenate([sorted_in[0, 2:4], sorted_in[1, 2:4]], axis=0),
-        jnp.concatenate([sorted_in[0, 4:6], sorted_in[1, 4:6]], axis=0),
+        jnp.concatenate([sorted_in[i, 2:4] for i in order_in], axis=0),
+        jnp.concatenate([sorted_in[i, 4:6] for i in order_in], axis=0),
         basis_in,
     )
-    for i, (present, device) in enumerate(sides):
+    for step, i in enumerate(order_in):
         for p in range(2):
             evaluate(
-                panel.at[p], basis_in, 2 * i + p, sorted_in[i, p : p + 1], raw_in[i, p], first_row,
-                parts, ghost_out.at[i, p],
+                panel[p], basis_in, 2 * step + p, sorted_in[i, p : p + 1], raw_in[i, p],
+                first_row, parts, ghost_out.at[i, p],
             )
-
-        @pl.when(present)
-        def _():
-            ghosts(i, device).start()
+        target = axial - 1 + 2 * i
+
+        @pl.when((target >= 0) & (target <= axial_last))
+        def _():
+            ghosts(i, {"axial": jnp.clip(target, 0, axial_last)}).start()
 
     def products(s):
         for t in range(TILES):
@@ -367,11 +395,16 @@
     def outside(i):
         for t in range(TILES):
             at = slice(t * TILE, (t + 1) * TILE)
-            x = stacked(halo[i, :, :, at].reshape(FP, TILE))
+            x = halo[i, :, :, at].reshape(FP, TILE)
+            x = jnp.concatenate([x, jnp.zeros_like(x), x, jnp.zeros((32, TILE), bf16)], axis=0)
             y = jnp.dot(stencil[FP : 2 * FP, :], x, preferred_element_type=f32)
             span_part[i * (LAYERS + 1), :, at] = y
 
     lane8 = lax.broadcasted_iota(jnp.int32, (8, 128), 1)
+
+    def lower_layer(f, t):
+        pair = halo[0, f, 16 * (t // 2) : 16 * (t // 2) + 16, :].astype(f32)
+        return pair[8 * (t % 2) : 8 * (t % 2) + 8]
 
     def combine(s):
         for t in range(PITCH // 8):
@@ -396,7 +429,7 @@
                     ],
                     axis=1,
                 )
-                lower = u[f, s - 1, r, :] if s else halo[0, f, r, :]
+                lower = u[f, s - 1, r, :] if s else lower_layer(f, t)
                 across = span_part[s + 2, rr, :] - span_part[s, rr, :] + 0.02 * lower
                 out[f, s, r, :] = (
                     keep * here + m[2] * pitch_part[slot(s), rr, :] + m[1] * across + m[0] * along
@@ -417,6 +450,12 @@
         @pl.when(present)
         def _():
             edges(1 - i, device).wait_recv()
+
+    for i, (present, device) in enumerate(((has_down, down), (has_up, up))):
+
+        @pl.when(present)
+        def _():
+            halos(1 - i, device).wait_recv()
 
     for i, sign in ((0, -0.01), (1, 0.01)):
         for f in range(FIELDS):
@@ -425,7 +464,10 @@
                 total = total + (-0.1 * jacobian[f, 0, g]) * edge_in[i, g]
             edge_add[i, f] = total
 
-    for s in range(2, LAYERS):
+    outside(0)
+    outside(1)
+    combine(0)
+    for s in range(2, 6):
         products(s)
         combine(s - 1)
 
@@ -448,18 +490,10 @@
             for g in range(FIELDS):
                 total = total + (sign * jacobian[f, 2, g]) * ghost[g * LAYERS : (g + 1) * LAYERS]
             fix[i, f] = scale * total
-    for s in range(1, LAYERS - 1):
-        patch(s)
-
-    for i, (present, device) in enumerate(((has_down, down), (has_up, up))):
-
-        @pl.when(present)
-        def _():
-            halos(1 - i, device).wait_recv()
-
-        outside(i)
-        s = 0 if i == 0 else LAYERS - 1
-        combine(s)
+        products(6 + i)
+        combine(5 + i)
+    combine(LAYERS - 1)
+    for s in range(LAYERS):
         patch(s)
 
     for i, (present, device) in enumerate(sides):
@@ -474,6 +508,16 @@
         @pl.when(present)
         def _():
             halos(i, device).wait_send()
+
+
+def store(held, out, sems):
+    copies = [
+        pltpu.make_async_copy(held.at[:, s], out.at[:, s], sems.at[s]) for s in range(LAYERS)
+    ]
+    for c in copies:
+        c.start()
+    for c in copies:
+        c.wait()
 
 
 def on_device(
@@ -486,19 +530,22 @@
     vmem = pl.BlockSpec(memory_space=pltpu.VMEM)
     anywhere = pl.BlockSpec(memory_space=pl.ANY)
     shape = (FIELDS, LAYERS, PITCH, ROWS)
-    return pl.pallas_call(
+    advanced = pl.pallas_call(
         kernel,
-        out_shape=jax.ShapeDtypeStruct(shape, f32),
-        in_specs=[vmem, vmem, vmem, pl.BlockSpec(memory_space=pltpu.SMEM)] + [anywhere] * 4,
+        out_shape=pltpu.VMEM(shape, f32),
+        in_specs=[anywhere] * 8,
         out_specs=vmem,
         scratch_shapes=[
             pltpu.VMEM(shape, f32),
             pltpu.VMEM((3, LAYERS, PITCH, ROWS), f32),
-            pltpu.VMEM((2, TILES, MODES * FS, TILE), bf16),
+            pltpu.VMEM((TILES, MODES * FS, TILE), bf16),
+            pltpu.VMEM((TILES, MODES * FS, TILE), bf16),
             pltpu.VMEM((2, ROWS, ROWS), bf16),
             pltpu.VMEM((8, ROWS), f32),
             pltpu.VMEM((2, 8, ROWS), f32),
             pltpu.VMEM((2, 8, 128), jnp.int32),
+            pltpu.VMEM((8, 128), f32),
+            pltpu.SMEM((FIELDS, 3, FIELDS), f32),
             pltpu.VMEM((2, 2, 8, 128), jnp.int32),
             pltpu.VMEM((TILES, MODES, 8, TILE), f32),
             pltpu.VMEM((TILES, MODES, 8, TILE), f32),
@@ -506,7 +553,8 @@
             pltpu.VMEM((2, FS, ROWS), f32),
             pltpu.VMEM((2, 2, FS, ROWS), f32),
             pltpu.VMEM((2, 2, FS, ROWS), f32),
-            pltpu.VMEM((2, FIELDS, PITCH, ROWS), f32),
+            pltpu.VMEM((2, FIELDS, PITCH, ROWS), bf16),
+            pltpu.VMEM((2, FIELDS, PITCH, ROWS), bf16),
             pltpu.VMEM((2, FIELDS, PITCH, 128), f32),
             pltpu.VMEM((2, FIELDS, PITCH, 128), f32),
             pltpu.VMEM((2, FIELDS, PITCH, 128), f32),
@@ -515,6 +563,7 @@
             pltpu.VMEM((5, FP, ROWS), f32),
             pltpu.VMEM((LAYERS + 2, FP, ROWS), f32),
             pltpu.VMEM((5, FP, ROWS), f32),
+            pltpu.SemaphoreType.DMA((4,)),
             pltpu.SemaphoreType.DMA((LAYERS,)),
             pltpu.SemaphoreType.DMA((LAYERS,)),
             pltpu.SemaphoreType.DMA((2, TILES)),
@@ -522,10 +571,19 @@
             pltpu.SemaphoreType.DMA((10,)),
         ],
         compiler_params=pltpu.CompilerParams(
-            collective_id=0, has_side_effects=True, vmem_limit_bytes=58 * 2**20
+            collective_id=0, has_side_effects=True, vmem_limit_bytes=50 * 2**20
         ),
         name="section",
     )(*rows, jacobian, conserved, metric, upper, lower)
+    return pl.pallas_call(
+        store,
+        out_shape=jax.ShapeDtypeStruct(shape, f32),
+        in_specs=[vmem],
+        out_specs=anywhere,
+        scratch_shapes=[pltpu.SemaphoreType.DMA((LAYERS,))],
+        compiler_params=pltpu.CompilerParams(vmem_limit_bytes=4 * 2**20),
+        name="store",
+    )(pltpu.with_memory_space_constraint(advanced, pltpu.VMEM))
 
 
 def solution(mesh):

time: 39.2 us -> 26.7 us (0.68)
  Pallas kernels: 33.3 us -> 26.4 us
  local copies, waits for them, and re-layouts: 5.7 us -> 0 us
    pallas_call x1 -> x2, Pallas kernels: 33.3 us -> 26.4 us  [the longest x1 24 us: on_device(): pl.pallas_call(kernel, out_shape=pltpu.VMEM(shape, f32), in_specs=[anywhe...]
    unnamed x1 -> x0, local copies, waits for them, and re-layouts: 5.7 us -> none
where the time goes in v1:
time: 26.7 us; the launch traced here: 26.6 us
  Pallas kernels  26.4 us (99%)
    pallas_call x1, Pallas kernels, on_device(): pl.pallas_call(kernel, out_shape=pltpu.VMEM(shape, f32), in_specs=[anywhe...  24 us
    pallas_call x1, Pallas kernels, on_device(): pl.pallas_call(store, out_shape=jax.ShapeDtypeStruct(shape, f32), in_spec...  2.42 us

profile of v1, /device:TPU:6, one launch (start us, length us, event | category | flops | bytes accessed | tf_op | source)
XLA Modules:
  0.0 26.6 jit_solution(3595888658631733844)
XLA Ops:
  0.0 24.0 %section.1.held = f32[5,8,32,1024]{3,2,1,0:T(8,128)S(1)} custom-call(s32[8,128]{1,0:T(8,128)} %bitcast.9, s32[8,128]{1,0:T(8,128)} %bitcast.10, f32[8,128]{1,0:T(8,128)} %bitcast.11, f32[5,3,5]{2,1,0:T(4,128)} %bitcast.8, f32[5,8,32,1024]{3,2,1,0:T(8,128)} %u_hbm.1, f32[3,8,32,1024]{3,2,1,0:T(8,128)} %metric_hbm.1, bf16[1280,1024]{1,0:T(8,128)(2,1)} %bitcast.6, ...), custom_call_target="tpu_custom_call" | custom-call | tf_op jit(solution)/shard_map/section/pallas_call | solution.py:533
  24.0 2.4 %store.1 = f32[5,8,32,1024]{3,2,1,0:T(8,128)} custom-call(f32[5,8,32,1024]{3,2,1,0:T(8,128)S(1)} %section.1.held), custom_call_target="tpu_custom_call" | custom-call | tf_op jit(solution)/shard_map/store/pallas_call | solution.py:578

commit v2 on v1

--- a/solution.py
+++ b/solution.py
@@ -18,6 +18,7 @@
 MODES = 32
 FS = FIELDS * LAYERS
 FP = FIELDS * PITCH
+HALF = PITCH // 2
 TILE = 256
 TILES = ROWS // TILE
 PAIRS = 2 * TILES - 1
@@ -129,21 +130,26 @@
         ghost[:, j * TILE : (j + 1) * TILE] = total
 
 
-def fill_stencil(jacobian, stencil):
-    column = lax.broadcasted_iota(jnp.int32, (PITCH, 512), 1)
-    row = lax.broadcasted_iota(jnp.int32, (PITCH, 512), 0)
-    third = jnp.where(column < FP, 0, jnp.where(column < 2 * FP, 1, jnp.where(column < 3 * FP, 2, 3)))
-    place = column - FP * third
-    field = jnp.where(third < 3, place // PITCH, -1)
-    cell = place % PITCH
+def fill_stencil(jacobian, directions, cells, stencil):
+    width = stencil.shape[1]
+    size = FIELDS * cells
+    column = lax.broadcasted_iota(jnp.int32, (cells, width), 1)
+    row = lax.broadcasted_iota(jnp.int32, (cells, width), 0)
+    third = jnp.where(
+        column < size, 0, jnp.where(column < 2 * size, 1, jnp.where(column < 3 * size, 2, 3))
+    )
+    place = column - size * third
+    field = jnp.where(third < 3, place // cells, -1)
+    cell = place % cells
     here = cell == row
     above = cell == row + 1
     below = cell == row - 1
-    for block, d in enumerate((2, 1, 0)):
+    for block, d in enumerate(directions):
         for f in range(FIELDS):
-            weight = jnp.zeros((PITCH, 512), f32)
+            weight = jnp.zeros((cells, width), f32)
             for g in range(FIELDS):
                 weight = jnp.where(field == g, -0.1 * jacobian[f, d, g], weight)
+            weight = jnp.where(third < 3, weight, 0.0)
             smooth = jnp.where(field == f, f32(0.01), f32(0.0))
             if d == 2:
                 value = jnp.where(above, smooth + weight, jnp.where(below, smooth - weight, 0.0))
@@ -151,13 +157,17 @@
                 value = jnp.where(here, smooth + weight, 0.0)
             high = value.astype(bf16).astype(f32)
             value = jnp.where(third == 2, value - high, high)
-            at = (block * FIELDS + f) * PITCH
-            stencil[at : at + PITCH, :] = value.astype(bf16)
-
-
-def stacked(x):
-    high, low = split2(x)
-    return jnp.concatenate([high, low, high, jnp.zeros((32, x.shape[1]), bf16)], axis=0)
+            at = (block * FIELDS + f) * cells
+            stencil[at : at + cells, :] = value.astype(bf16)
+
+
+def stacked(high, low, first, cells):
+    def part(x):
+        return [x[PITCH * g + first : PITCH * g + first + cells] for g in range(FIELDS)]
+
+    pad = -3 * FIELDS * cells % TILE
+    rows = part(high) + part(low) + part(high) + [jnp.zeros((pad, high.shape[1]), bf16)]
+    return jnp.concatenate(rows, axis=0)
 
 
 def slot(s):
@@ -197,7 +207,8 @@
     edge_in,
     edge_add,
     fix,
-    stencil,
+    pitch_matrix,
+    side_matrix,
     pitch_part,
     span_part,
     axial_part,
@@ -324,7 +335,8 @@
         def _():
             halos(i, device).start()
 
-    fill_stencil(jacobian, stencil)
+    fill_stencil(jacobian, (2,), PITCH, pitch_matrix)
+    fill_stencil(jacobian, (1, 0), HALF, side_matrix)
     fill_basis(sorted_own[2:4], sorted_own[4:6], basis_own)
 
     first_row = axial * ROWS
@@ -386,19 +398,31 @@
     def products(s):
         for t in range(TILES):
             at = slice(t * TILE, (t + 1) * TILE)
-            x = stacked(u[:, s, :, at].reshape(FP, TILE))
-            y = jnp.dot(stencil[...], x, preferred_element_type=f32)
-            pitch_part[slot(s), :, at] = y[0:FP]
-            span_part[s + 1, :, at] = y[FP : 2 * FP]
-            axial_part[slot(s), :, at] = y[2 * FP : 3 * FP]
+            high, low = split2(u[:, s, :, at].reshape(FP, TILE))
+            x = stacked(high, low, 0, PITCH)
+            pitch_part[slot(s), :, at] = jnp.dot(
+                pitch_matrix[...], x, preferred_element_type=f32
+            )
+            for first in (0, HALF):
+                x = stacked(high, low, first, HALF)
+                y = jnp.dot(side_matrix[...], x, preferred_element_type=f32)
+                for f in range(FIELDS):
+                    r = slice(PITCH * f + first, PITCH * f + first + HALF)
+                    span_part[s + 1, r, at] = y[HALF * f : HALF * (f + 1)]
+                    axial_part[slot(s), r, at] = y[HALF * (FIELDS + f) : HALF * (FIELDS + f + 1)]
 
     def outside(i):
         for t in range(TILES):
             at = slice(t * TILE, (t + 1) * TILE)
-            x = halo[i, :, :, at].reshape(FP, TILE)
-            x = jnp.concatenate([x, jnp.zeros_like(x), x, jnp.zeros((32, TILE), bf16)], axis=0)
-            y = jnp.dot(stencil[FP : 2 * FP, :], x, preferred_element_type=f32)
-            span_part[i * (LAYERS + 1), :, at] = y
+            high = halo[i, :, :, at].reshape(FP, TILE)
+            for first in (0, HALF):
+                x = stacked(high, jnp.zeros_like(high), first, HALF)
+                y = jnp.dot(
+                    side_matrix[0 : FIELDS * HALF, :], x, preferred_element_type=f32
+                )
+                for f in range(FIELDS):
+                    r = slice(PITCH * f + first, PITCH * f + first + HALF)
+                    span_part[i * (LAYERS + 1), r, at] = y[HALF * f : HALF * (f + 1)]
 
     lane8 = lax.broadcasted_iota(jnp.int32, (8, 128), 1)
 
@@ -451,12 +475,6 @@
         def _():
             edges(1 - i, device).wait_recv()
 
-    for i, (present, device) in enumerate(((has_down, down), (has_up, up))):
-
-        @pl.when(present)
-        def _():
-            halos(1 - i, device).wait_recv()
-
     for i, sign in ((0, -0.01), (1, 0.01)):
         for f in range(FIELDS):
             total = sign * edge_in[i, f]
@@ -464,9 +482,6 @@
                 total = total + (-0.1 * jacobian[f, 0, g]) * edge_in[i, g]
             edge_add[i, f] = total
 
-    outside(0)
-    outside(1)
-    combine(0)
     for s in range(2, 6):
         products(s)
         combine(s - 1)
@@ -476,6 +491,12 @@
         @pl.when(present)
         def _():
             ghosts(1 - i, device).wait_recv()
+
+    for i, (present, device) in enumerate(((has_down, down), (has_up, up))):
+
+        @pl.when(present)
+        def _():
+            halos(1 - i, device).wait_recv()
 
     for i, (p, sign) in enumerate(((0, 0.1), (PITCH - 1, -0.1))):
         total = ghost_own[i] + ghost_in[0, i] + ghost_in[1, i]
@@ -490,8 +511,10 @@
             for g in range(FIELDS):
                 total = total + (sign * jacobian[f, 2, g]) * ghost[g * LAYERS : (g + 1) * LAYERS]
             fix[i, f] = scale * total
+        outside(i)
         products(6 + i)
         combine(5 + i)
+    combine(0)
     combine(LAYERS - 1)
     for s in range(LAYERS):
         patch(s)
@@ -559,7 +582,8 @@
             pltpu.VMEM((2, FIELDS, PITCH, 128), f32),
             pltpu.VMEM((2, FIELDS, PITCH, 128), f32),
             pltpu.VMEM((2, FIELDS, LAYERS, ROWS), f32),
-            pltpu.VMEM((3 * FP, 512), bf16),
+            pltpu.VMEM((FP, 512), bf16),
+            pltpu.VMEM((2 * FIELDS * HALF, TILE), bf16),
             pltpu.VMEM((5, FP, ROWS), f32),
             pltpu.VMEM((LAYERS + 2, FP, ROWS), f32),
             pltpu.VMEM((5, FP, ROWS), f32),

time: 26.7 us -> 25.8 us (0.966)
  Pallas kernels: 26.4 us -> 25.5 us
    pallas_call x1, Pallas kernels: 24 us -> 23.1 us  [on_device(): pl.pallas_call(kernel, out_shape=pltpu.VMEM(shape, f32), in_specs=[anywhe...]
where the time goes in v2:
time: 25.8 us; the launch traced here: 25.7 us
  Pallas kernels  25.5 us (99%)
    pallas_call x1, Pallas kernels, on_device(): pl.pallas_call(kernel, out_shape=pltpu.VMEM(shape, f32), in_specs=[anywhe...  23.1 us
    pallas_call x1, Pallas kernels, on_device(): pl.pallas_call(store, out_shape=jax.ShapeDtypeStruct(shape, f32), in_spec...  2.42 us

profile of v2, /device:TPU:6, one launch (start us, length us, event | category | flops | bytes accessed | tf_op | source)
XLA Modules:
  0.0 25.7 jit_solution(8327232923847627911)
XLA Ops:
  0.0 23.1 %section.1.held = f32[5,8,32,1024]{3,2,1,0:T(8,128)S(1)} custom-call(s32[8,128]{1,0:T(8,128)} %bitcast.9, s32[8,128]{1,0:T(8,128)} %bitcast.10, f32[8,128]{1,0:T(8,128)} %bitcast.11, f32[5,3,5]{2,1,0:T(4,128)} %bitcast.8, f32[5,8,32,1024]{3,2,1,0:T(8,128)} %u_hbm.1, f32[3,8,32,1024]{3,2,1,0:T(8,128)} %metric_hbm.1, bf16[1280,1024]{1,0:T(8,128)(2,1)} %bitcast.6, ...), custom_call_target="tpu_custom_call" | custom-call | tf_op jit(solution)/shard_map/section/pallas_call | solution.py:556
  23.1 2.4 %store.1 = f32[5,8,32,1024]{3,2,1,0:T(8,128)} custom-call(f32[5,8,32,1024]{3,2,1,0:T(8,128)S(1)} %section.1.held), custom_call_target="tpu_custom_call" | custom-call | tf_op jit(solution)/shard_map/store/pallas_call | solution.py:602

commit v3 on v2

--- a/solution.py
+++ b/solution.py
@@ -262,7 +262,7 @@
             )
         )
     ]
-    for c in small + ends + panel_copies[:TILES]:
+    for c in small + panel_copies[:TILES] + ends:
         c.start()
 
     for i, (present, _) in enumerate(sides):
@@ -290,11 +290,6 @@
 
     for c in panel_copies[TILES:]:
         c.start()
-    for c in ends:
-        c.wait()
-    halo_out[0] = u[:, 0].astype(bf16)
-    halo_out[1] = u[:, LAYERS - 1].astype(bf16)
-
     pl.semaphore_wait(barrier, sum(present.astype(jnp.int32) for present, _ in around))
 
     def remote(number, source, target, device):
@@ -328,6 +323,11 @@
         def _():
             for c in tables(i, device):
                 c.start()
+
+    for c in ends:
+        c.wait()
+    halo_out[0] = u[:, 0].astype(bf16)
+    halo_out[1] = u[:, LAYERS - 1].astype(bf16)
 
     for i, (present, device) in enumerate(((has_down, down), (has_up, up))):
 

time: 25.8 us -> 25.8 us (level)
  no operation moved by 1% of the time
where the time goes in v3:
time: 25.8 us; the launch traced here: 25.7 us
  Pallas kernels  25.5 us (99%)
    pallas_call x1, Pallas kernels, on_device(): pl.pallas_call(kernel, out_shape=pltpu.VMEM(shape, f32), in_specs=[anywhe...  23.1 us
    pallas_call x1, Pallas kernels, on_device(): pl.pallas_call(store, out_shape=jax.ShapeDtypeStruct(shape, f32), in_spec...  2.42 us

profile of v3, /device:TPU:6, one launch (start us, length us, event | category | flops | bytes accessed | tf_op | source)
XLA Modules:
  0.0 25.7 jit_solution(4611054388352699830)
XLA Ops:
  0.0 23.1 %section.1.held = f32[5,8,32,1024]{3,2,1,0:T(8,128)S(1)} custom-call(s32[8,128]{1,0:T(8,128)} %bitcast.9, s32[8,128]{1,0:T(8,128)} %bitcast.10, f32[8,128]{1,0:T(8,128)} %bitcast.11, f32[5,3,5]{2,1,0:T(4,128)} %bitcast.8, f32[5,8,32,1024]{3,2,1,0:T(8,128)} %u_hbm.1, f32[3,8,32,1024]{3,2,1,0:T(8,128)} %metric_hbm.1, bf16[1280,1024]{1,0:T(8,128)(2,1)} %bitcast.6, ...), custom_call_target="tpu_custom_call" | custom-call | tf_op jit(solution)/shard_map/section/pallas_call | solution.py:556
  23.1 2.4 %store.1 = f32[5,8,32,1024]{3,2,1,0:T(8,128)} custom-call(f32[5,8,32,1024]{3,2,1,0:T(8,128)S(1)} %section.1.held), custom_call_target="tpu_custom_call" | custom-call | tf_op jit(solution)/shard_map/store/pallas_call | solution.py:602
